TPU v7x, 32 devices: a whole 2x2x4 slice. The times are simulated.
32 devices in a mesh: seq: 16 (over z, y, x), head: 2 (over core).
Axes of the slice: x: 2, y: 2, z: 4, core: 2. Of those that a mesh axis runs over, the one named last changes fastest.
Arguments:
- q_lin: bfloat16 [4096, 512], P('seq', 'head'), may hold values from -6 to 6
- k_lin: bfloat16 [4096, 512], P('seq', 'head'), may hold values from -6 to 6
- v_lin: bfloat16 [4096, 512], P('seq', 'head'), may hold values from -6 to 6
- log_decay: float32 [4, 4096], P('head', 'seq'), may hold values from -0.4 to 0, as said below
- q_soft: bfloat16 [4096, 512], P('seq', 'head'), may hold values from -12 to 12
- k_soft: bfloat16 [4096, 512], P('seq', 'head'), may hold values from -6 to 6
- v_soft: bfloat16 [4096, 512], P('seq', 'head'), may hold values from -6 to 6
- wo_lin: bfloat16 [512, 4096], P('head'), may hold values from -0.375 to 0.375
- wo_soft: bfloat16 [512, 4096], P('head'), may hold values from -0.375 to 0.375
Outputs:
- lin_mixed: bfloat16 [4096, 4096], P('seq', 'head')
- soft_mixed: bfloat16 [4096, 4096], P('seq', 'head')
Inputs may be any that keep to these rules, and one draw needn't show every extreme that they name: `log_decay`: log decays are never positive.
All inputs are finite; a program needn't handle non-finite values.
Results may differ from a plain program's by a relative error of at most 0.012.
Values may be sent and summed in bfloat16 or wider, within the bound.
A program may use at most 64 MiB of HBM per device.

v0:
```python
import math
import jax
import jax.numpy as jnp
from jax import lax
from jax.sharding import PartitionSpec as P

HIGHEST = lax.Precision.HIGHEST
NEG_BIG = -1e30


def prefix(shard, axis, combine, identity):
    size, here = (lax.axis_size(axis), lax.axis_index(axis))
    everything = jax.tree.map(
        lambda part, kind: lax.all_gather(part.astype(kind), axis),
        shard,
        (jnp.bfloat16, jnp.bfloat16),
    )
    start = jax.tree.map(
        lambda part, zero: jnp.broadcast_to(jnp.asarray(zero, part.dtype), part.shape),
        shard,
        identity,
    )

    def turn(k, before):
        reached = k < here
        new = combine(
            before, jax.tree.map(lambda part, own: part[k].astype(own.dtype), everything, shard)
        )
        return jax.tree.map(lambda a, b: jnp.where(reached, a, b), new, before)

    return lax.fori_loop(0, size, turn, start)


def second_half(device):
    return 2 * device + 1


def absorb(state, query_half, key_block, value_block, allowed, factor):
    row_top, row_sum, weighted = state
    scores = (
        jnp.einsum("qhd,khd->hqk", query_half, key_block, preferred_element_type=jnp.float32)
        * factor
    )
    if allowed is not None:
        scores = jnp.where(allowed[None], scores, -jnp.inf)
    new_top = jnp.maximum(row_top, jnp.max(scores, axis=-1))
    shrink = jnp.exp(row_top - new_top)
    weights = jnp.exp(scores - new_top[:, :, None])
    row_sum = row_sum * shrink + jnp.sum(weights, axis=-1)
    weighted = weighted * shrink.T[:, :, None] + jnp.einsum(
        "hqk,khd->qhd",
        weights.astype(jnp.bfloat16),
        value_block,
        preferred_element_type=jnp.float32,
    )
    return (new_top, row_sum, weighted)


def lightning_heads(q_lin, k_lin, v_lin, log_decay):
    row_count = q_lin.shape[0]
    head_count = log_decay.shape[0]
    head_width = q_lin.shape[1] // head_count
    query_plain = q_lin.reshape(row_count, head_count, head_width)
    key_plain = k_lin.reshape(row_count, head_count, head_width)
    queries = query_plain.astype(jnp.float32)
    key_rows = key_plain.astype(jnp.float32)
    values = v_lin.astype(jnp.float32).reshape(row_count, head_count, head_width)
    cumulative = jnp.cumsum(log_decay, axis=1)
    lower = jnp.arange(row_count)[:, None] >= jnp.arange(row_count)[None, :]
    decay_gap = jnp.where(lower[None], cumulative[:, :, None] - cumulative[:, None, :], -jnp.inf)
    scores = jnp.einsum(
        "thd,shd->hts", query_plain, key_plain, preferred_element_type=jnp.float32
    ) * jnp.exp(decay_gap)
    inside = jnp.einsum("hts,shd->thd", scores, values, precision=HIGHEST)
    closing = jnp.exp(cumulative[:, -1:] - cumulative)
    own_state = jnp.einsum(
        "shd,she->hde", key_rows * closing.T[:, :, None], values, precision=HIGHEST
    )
    own_decay = cumulative[:, -1]

    def combine(earlier, later):
        return (jnp.exp(later[1])[:, None, None] * earlier[0] + later[0], earlier[1] + later[1])

    identity = (jnp.zeros_like(own_state), jnp.zeros_like(own_decay))
    carried, _ = prefix((own_state, own_decay), "seq", combine, identity)
    from_before = (
        jnp.einsum("thd,hde->the", queries, carried, precision=HIGHEST)
        * jnp.exp(cumulative).T[:, :, None]
    )
    raw = inside + from_before
    factor = lax.rsqrt(jnp.mean(raw * raw, axis=-1, keepdims=True) + 1e-06)
    return (raw * factor).astype(jnp.bfloat16).reshape(row_count, head_count * head_width)


def softmax_heads(q_soft, k_soft, v_soft, head_width):
    row_count = q_soft.shape[0]
    half_rows = row_count // 2
    head_count = q_soft.shape[1] // head_width
    own_index = lax.axis_index("seq")
    factor = 1.0 / math.sqrt(head_width)
    shaped = q_soft.reshape(2, half_rows, head_count, head_width)
    query_ids = (2 * own_index, second_half(own_index))
    triangle = jnp.arange(half_rows)[:, None] >= jnp.arange(half_rows)[None, :]

    def block_pass(state, side, key_block, value_block, key_id):

        def full_block(inner_state):
            return absorb(inner_state, shaped[side], key_block, value_block, None, factor)

        def diagonal_block(inner_state):
            return absorb(inner_state, shaped[side], key_block, value_block, triangle, factor)

        def skipped(inner_state):
            return inner_state

        def not_below(inner_state):
            return lax.cond(key_id == query_ids[side], diagonal_block, skipped, inner_state)

        return lax.cond(key_id < query_ids[side], full_block, not_below, state)

    start_state = tuple(
        (
            (
                jnp.full((head_count, half_rows), NEG_BIG, jnp.float32),
                jnp.zeros((head_count, half_rows), jnp.float32),
                jnp.zeros((half_rows, head_count, head_width), jnp.float32),
            )
            for side in range(2)
        )
    )
    carry = start_state
    key_piece = lax.all_gather(k_soft, "seq", axis=0, tiled=True)
    value_piece = lax.all_gather(v_soft, "seq", axis=0, tiled=True)
    piece_rows = key_piece.shape[0]
    blocks = piece_rows // half_rows
    key_blocks = key_piece.reshape(blocks, half_rows, head_count, head_width)
    value_blocks = value_piece.reshape(blocks, half_rows, head_count, head_width)
    firsts = half_rows * jnp.arange(blocks, dtype=jnp.int32)

    def inner(state, block_item):
        key_block, value_block, first = block_item
        key_id = first // half_rows
        return (
            tuple(
                (block_pass(state[side], side, key_block, value_block, key_id) for side in range(2))
            ),
            None,
        )

    carry, _ = lax.scan(inner, carry, (key_blocks, value_blocks, firsts))
    halves = [
        (carry[side][2] / carry[side][1].T[:, :, None])
        .astype(jnp.bfloat16)
        .reshape(half_rows, head_count * head_width)
        for side in range(2)
    ]
    return jnp.concatenate(halves, axis=0)


def local(q_lin, k_lin, v_lin, log_decay, q_soft, k_soft, v_soft, wo_lin, wo_soft):
    head_width = q_lin.shape[1] // log_decay.shape[0]
    lin_out = lightning_heads(q_lin, k_lin, v_lin, log_decay)
    soft_out = softmax_heads(q_soft, k_soft, v_soft, head_width)
    lin_term = jnp.dot(lin_out, wo_lin, preferred_element_type=jnp.float32)
    soft_term = jnp.dot(soft_out, wo_soft, preferred_element_type=jnp.float32)
    lin_sum, soft_sum = (
        lax.psum_scatter(
            lin_term.astype(jnp.bfloat16).astype(jnp.float32).astype(jnp.bfloat16),
            "head",
            scatter_dimension=1,
            tiled=True,
        ).astype(jnp.float32),
        lax.psum_scatter(
            soft_term.astype(jnp.bfloat16).astype(jnp.float32).astype(jnp.bfloat16),
            "head",
            scatter_dimension=1,
            tiled=True,
        ).astype(jnp.float32),
    )
    return (lin_sum.astype(jnp.bfloat16), soft_sum.astype(jnp.bfloat16))


def solution(mesh):
    in_specs = (
        P("seq", "head"),
        P("seq", "head"),
        P("seq", "head"),
        P("head", "seq"),
        P("seq", "head"),
        P("seq", "head"),
        P("seq", "head"),
        P("head", None),
        P("head", None),
    )
    out_specs = (P("seq", "head"), P("seq", "head"))
    return jax.shard_map(local, mesh=mesh, in_specs=in_specs, out_specs=out_specs, check_vma=False)
```

profile of v0, /device:TPU:0, one launch (start us, length us, event | category | flops | bytes accessed | tf_op | source)
XLA Modules:
  0.0 389.1 jit_solution(17133437121583700277)
XLA Ops:
  9.3 1.0 copy.69
  10.4 1.8 convolution_convert_fusion.2
  13.8 1.2 dynamic-slice
  15.9 43.7 %all-reduce = bf16[32]{0:T(256)(128)(2,1)S(1)} all-reduce(bf16[32]{0:T(256)(128)(2,1)S(1)} %dynamic-update-slice), channel_id=2, replica_groups=mesh['seq'=16,'head'=2] {'seq'}, use_global_device_ids=true, to_apply=%add | all-reduce | flops 32 | bytes 128
  60.7 1.1 convolution_multiply_fusion.4
  61.8 8.6 %all-gather.10.cloned.1.call-done = bf16[32,128,128]{2,1,0:T(8,128)(2,1)} async-done(((bf16[2,128,128]{2,1,0:T(8,128)(2,1)}), bf16[32,128,128]{2,1,0:T(8,128)(2,1)}) %all-gather.10.cloned.1.call-update) | async-done | bytes 1048592 | tf_op jit(solution)/shard_map/all_gather | solution.py:14
  70.5 15.6 %while.39 = (s32[]{:T(128)}, f32[2,128,128]{2,1,0:T(8,128)S(1)}, s32[]{:T(128)}, bf16[16,2]{1,0:T(8,128)(2,1)S(1)}, bf16[16,2,128,128]{3,2,1,0:T(8,128)(2,1)}, /*index=5*/s32[]{:T(128)}, s32[]{:T(128)}) while((s32[]{:T(128)}, f32[2,128,128]{2,1,0:T(8,128)S(1)}, s32[]{:T(128)}, bf16[16,2]{1,0:T(8,128)(2,1)S(1)}, ...), condition=%wide.region_3.4_spmd.clone, body=%wide.region_2.3_spmd.clone.sunk | while | flops 163846 | bytes 327813 | solution.py:31
  86.9 2.1 convolution_convert_fusion.1
  89.1 43.7 %all-gather.6.cloned.1.call-done = bf16[4096,256]{1,0:T(8,128)(2,1)} async-done(((bf16[256,256]{1,0:T(8,128)(2,1)}), bf16[4096,256]{1,0:T(8,128)(2,1)}) %all-gather.6.cloned.1.call-update) | async-done | bytes 2097168 | tf_op jit(solution)/shard_map/all_gather | solution.py:132
  132.8 4.0 %reshape.143 = bf16[32,128,2,128]{3,2,1,0:T(2,128)(2,1)} reshape(bf16[4096,256]{1,0:T(8,128)(2,1)} %all-gather.6.cloned.1.call-done) | data formatting | bytes 4194304 | tf_op jit(solution)/shard_map/reshape | solution.py:136
  136.8 58.2 %all-gather.8.cloned.1.call-done = bf16[4096,256]{1,0:T(8,128)(2,1)} async-done(((bf16[256,256]{1,0:T(8,128)(2,1)}), bf16[4096,256]{1,0:T(8,128)(2,1)}) %all-gather.8.cloned.1.call-update) | async-done | bytes 2097168 | tf_op jit(solution)/shard_map/all_gather | solution.py:133
  195.0 4.0 %reshape.144 = bf16[32,128,2,128]{3,2,1,0:T(2,128)(2,1)} reshape(bf16[4096,256]{1,0:T(8,128)(2,1)} %all-gather.8.cloned.1.call-done) | data formatting | bytes 4194304 | tf_op jit(solution)/shard_map/reshape | solution.py:137
  199.0 141.2 %while.38 = (s32[]{:T(128)}, f32[2,128]{1,0:T(2,128)S(1)}, f32[2,128]{1,0:T(2,128)S(1)}, f32[128,2,128]{2,0,1:T(8,128)S(1)}, f32[2,128]{1,0:T(2,128)S(1)}, /*ind...) while((s32[]{:T(128)}, f32[2,128]{1,0:T(2,128)S(1)}, ...), condition=%wide.region_23.24_spmd.clone.clone, body=%wide.region_6.23_spmd.clone.clone.sunk | while | flops 34162200 | bytes 2311003 | solution.py:150
  202.3 1.0 constant_dynamic-slice_fusion.3
  207.7 1.0 constant_dynamic-slice_fusion.3
  212.6 1.0 constant_dynamic-slice_fusion.3
  216.9 1.0 constant_dynamic-slice_fusion.3
  221.3 1.0 constant_dynamic-slice_fusion.3
  225.7 1.0 constant_dynamic-slice_fusion.3
  230.0 1.0 constant_dynamic-slice_fusion.3
  234.4 1.0 constant_dynamic-slice_fusion.3
  238.7 1.0 constant_dynamic-slice_fusion.3
  243.1 1.0 constant_dynamic-slice_fusion.3
  247.5 1.0 constant_dynamic-slice_fusion.3
  251.8 1.0 constant_dynamic-slice_fusion.3
  256.2 1.0 constant_dynamic-slice_fusion.3
  260.5 1.0 constant_dynamic-slice_fusion.3
  264.9 1.0 constant_dynamic-slice_fusion.3
  269.3 1.0 constant_dynamic-slice_fusion.3
  273.6 1.0 constant_dynamic-slice_fusion.3
  340.4 3.6 convolution_convert_fusion
  344.1 38.5 %reduce-scatter.5.cloned.1.call-done = bf16[256,2048]{1,0:T(8,128)(2,1)} async-done(((bf16[256,4096]{1,0:T(8,128)(2,1)}), bf16[256,2048]{1,0:T(8,128)(2,1)}) %reduce-scatter.5.cloned.1.call-update) | async-done | bytes 1048592 | tf_op jit(solution)/shard_map/reduce_scatter | solution.py:173
  (369 shorter events, 63.6 us)
Async XLA Ops:
  7.2 79.8 %copy-start = (bf16[256,4096]{1,0:T(8,128)(2,1)S(1)}, bf16[256,4096]{1,0:T(8,128)(2,1)}, u32[]{:S(2)}) copy-start(bf16[256,4096]{1,0:T(8,128)(2,1)} %param.28) | copy-start | bytes 6291460
  7.2 63.3 %all-gather.10.cloned.1.call-start = ((), (), s32[]{:S(2)}) async-start(), calls=%async_computation.6 | async-start | bytes 1114112 | tf_op jit(solution)/shard_map/all_gather | solution.py:14
  10.3 75.7 %copy-start.2 = (bf16[256,256]{1,0:T(8,128)(2,1)S(1)}, bf16[256,256]{1,0:T(8,128)(2,1)}, u32[]{:S(2)}) copy-start(bf16[256,256]{1,0:T(8,128)(2,1)} %param.21) | copy-start | bytes 393220
  12.2 120.6 %all-gather.6.cloned.1.call-start = ((), (), s32[]{:S(2)}) async-start(), calls=%async_computation.3 | async-start | bytes 2228224 | tf_op jit(solution)/shard_map/all_gather | solution.py:132
  13.0 73.4 %copy-start.1 = (bf16[256,256]{1,0:T(8,128)(2,1)S(1)}, bf16[256,256]{1,0:T(8,128)(2,1)}, u32[]{:S(2)}) copy-start(bf16[256,256]{1,0:T(8,128)(2,1)} %param.23) | copy-start | bytes 393220
  13.0 182.0 %all-gather.8.cloned.1.call-start = ((), (), s32[]{:S(2)}) async-start(), calls=%async_computation.4 | async-start | bytes 2228224 | tf_op jit(solution)/shard_map/all_gather | solution.py:133
  13.7 330.4 %reduce-scatter.3.cloned.1.call-start = ((), (), s32[]{:S(2)}) async-start(), calls=%async_computation.2 | async-start | bytes 3145728 | tf_op jit(solution)/shard_map/reduce_scatter | solution.py:167
  89.0 293.5 %reduce-scatter.5.cloned.1.call-start = ((), (), s32[]{:S(2)}) async-start(), calls=%async_computation.5 | async-start | bytes 3145728 | tf_op jit(solution)/shard_map/reduce_scatter | solution.py:173
Sparse Core Ops, SparseCore 0:
  12.3 58.0 all-gather.9
  73.2 59.5 all-gather.5
  135.6 59.3 all-gather.7
  197.6 8.2 reduce-scatter.2
  344.2 38.3 reduce-scatter.4
where the time goes:
time: 393 us; the launch traced here: 389 us
  waiting for transfers between devices  150 us (38%)
  loops' own time  89.1 us (23%)
  local copies, waits for them, and re-layouts  63.5 us (16%)
  blocking collectives  43.7 us (11%)
  other arithmetic  16.9 us (4%)
  between operations  14.6 us (4%)
  matrix products  10.7 us (3%)
    another operation x1, loops' own time, softmax_heads(): carry, _ = lax.scan(inner, carry, (key_blocks, value_blocks, firsts))  85.6 us
    all_gather x1, waiting for transfers between devices, softmax_heads(): value_piece = lax.all_gather(v_soft, 'seq', axis=0, tiled=True)  58.2 us
    dynamic_slice x128, local copies, waits for them, and re-layouts, softmax_heads(): carry, _ = lax.scan(inner, carry, (key_blocks, value_blocks, firsts))  50.6 us
    all_gather x1, waiting for transfers between devices, softmax_heads(): key_piece = lax.all_gather(k_soft, 'seq', axis=0, tiled=True)  43.7 us
    unnamed x1, blocking collectives  43.7 us
    reduce_scatter x1, waiting for transfers between devices, local(): lax.psum_scatter(soft_term.astype(jnp.bfloat16).astype(jnp.float32).astyp...  38.5 us
    select_n x16, other arithmetic, turn(): return jax.tree.map(lambda a, b: jnp.where(reached, a, b), new, before)  14.9 us
    all_gather x1, waiting for transfers between devices, prefix(): lax.all_gather(part.astype(kind), axis)  8.65 us
  transfers between devices with their start and end apart: 5, of which 4 were waited for; matrix products, arithmetic and copies ran while one was open for 22% of the time, Pallas kernels for 0%

commit v1 on v0

--- a/solution.py
+++ b/solution.py
@@ -129,7 +129,38 @@
         )
     )
     carry = start_state
-    key_piece = lax.all_gather(k_soft, "seq", axis=0, tiled=True)
+
+    def close_pieces_all(message):
+        group_axis = "seq"
+        p_next = jax.lax.axis_size(group_axis)
+        met_up, arr_out, response = (p_next, jax.lax.axis_index(group_axis), message.shape[0])
+        small = big = message
+        v_next = lax.dynamic_update_slice_in_dim(
+            jnp.zeros(
+                [jj * met_up if at == 0 else jj for at, jj in enumerate(message.shape)],
+                message.dtype,
+            ),
+            message,
+            arr_out * response,
+            axis=0,
+        )
+        for u in range(1, met_up // 2 + 1):
+            small = jax.lax.ppermute(
+                small, group_axis, perm=list(map(lambda at: (at, (at + 1) % met_up), range(met_up)))
+            )
+            v_next = lax.dynamic_update_slice_in_dim(
+                v_next, small, (arr_out - u) % met_up * response, axis=0
+            )
+            if 2 * u < met_up:
+                out_arr = range(met_up)
+                a_next = map(lambda at: (at, (at - 1) % met_up), out_arr)
+                big = jax.lax.ppermute(big, group_axis, perm=list(a_next))
+                v_next = lax.dynamic_update_slice_in_dim(
+                    v_next, big, (arr_out + u) % met_up * response, axis=0
+                )
+        return v_next
+
+    key_piece = close_pieces_all(k_soft)
     value_piece = lax.all_gather(v_soft, "seq", axis=0, tiled=True)
     piece_rows = key_piece.shape[0]
     blocks = piece_rows // half_rows

time: 393 us -> 381 us (0.969)
  waiting for transfers between devices: 150 us -> 58 us
  starting transfers between devices: 0.2 us -> 42.6 us
  local copies, waits for them, and re-layouts: 63.5 us -> 105 us
  blocking collectives: 43.7 us -> 38.6 us
    all_gather x1, waiting for transfers between devices: 58.2 us -> 0.02 us  [softmax_heads(): value_piece = lax.all_gather(v_soft, 'seq', axis=0, tiled=True)]
    all_gather x1 -> x0, waiting for transfers between devices: 43.7 us -> none  [softmax_heads(): key_piece = lax.all_gather(k_soft, 'seq', axis=0, tiled=True)]
    ppermute x0 -> x15, starting transfers between devices: none -> 42.5 us  [the longest x7 38.7 us: close_pieces_all(): big = jax.lax.ppermute(big, group_axis, perm=list(a_next))]
    squeeze x0 -> x32, local copies, waits for them, and re-layouts: none -> 27.6 us  [softmax_heads(): carry, _ = lax.scan(inner, carry, (key_blocks, value_blocks, firsts))]
    ppermute x0 -> x15, waiting for transfers between devices: none -> 22.5 us  [the longest x8 18.2 us: close_pieces_all(): jax.lax.ppermute(small, group_axis, perm=list(map(lambda at: (at, (at + 1...]
    dynamic_update_slice x0 -> x16, local copies, waits for them, and re-layouts: none -> 11 us  [the longest x8 5.51 us: close_pieces_all(): lax.dynamic_update_slice_in_dim(v_next, small, (arr_out - u) % met_up * r...]
    all_gather x1, waiting for transfers between devices: 8.65 us -> 0.01 us  [prefix(): lax.all_gather(part.astype(kind), axis)]
    unnamed x12 -> x19, local copies, waits for them, and re-layouts: 1.61 us -> 9.67 us
  transfers between devices with their start and end apart: 5 -> 19, of which waited for: 4 -> 11; matrix products, arithmetic and copies ran while one was open for 22% -> 34% of each run, Pallas kernels for 0% -> 0%
where the time goes in v1:
time: 381 us; the launch traced here: 375 us
  local copies, waits for them, and re-layouts  105 us (28%)
  loops' own time  88.5 us (23%)
  waiting for transfers between devices  58 us (15%)
  starting transfers between devices  42.6 us (11%)
  blocking collectives  38.6 us (10%)
  other arithmetic  16.8 us (4%)
  between operations  14.8 us (4%)
  matrix products  10.7 us (3%)
    another operation x1, loops' own time, softmax_heads(): carry, _ = lax.scan(inner, carry, (key_blocks, value_blocks, firsts))  85.2 us
    dynamic_slice x64, local copies, waits for them, and re-layouts, softmax_heads(): carry, _ = lax.scan(inner, carry, (key_blocks, value_blocks, firsts))  47.3 us
    ppermute x7, starting transfers between devices, close_pieces_all(): big = jax.lax.ppermute(big, group_axis, perm=list(a_next))  38.7 us
    unnamed x1, blocking collectives  38.6 us
    reduce_scatter x1, waiting for transfers between devices, local(): lax.psum_scatter(soft_term.astype(jnp.bfloat16).astype(jnp.float32).astyp...  35.3 us
    squeeze x32, local copies, waits for them, and re-layouts, softmax_heads(): carry, _ = lax.scan(inner, carry, (key_blocks, value_blocks, firsts))  27.6 us
    ppermute x8, waiting for transfers between devices, close_pieces_all(): jax.lax.ppermute(small, group_axis, perm=list(map(lambda at: (at, (at + 1...  18.2 us
    select_n x16, other arithmetic, turn(): return jax.tree.map(lambda a, b: jnp.where(reached, a, b), new, before)  14.9 us
  transfers between devices with their start and end apart: 19, of which 11 were waited for; matrix products, arithmetic and copies ran while one was open for 34% of the time, Pallas kernels for 0%

profile of v1, /device:TPU:0, one launch (start us, length us, event | category | flops | bytes accessed | tf_op | source)
XLA Modules:
  0.0 375.4 jit_solution(9353158057811611917)
XLA Ops:
  9.3 1.0 copy.96
  10.3 1.8 convolution_convert_fusion.2
  12.2 3.0 collective-permute-start
  15.2 4.1 %collective-permute-start.1 = (bf16[256,256]{1,0:T(8,128)(2,1)}, bf16[256,256]{1,0:T(8,128)(2,1)S(1)}, u32[]{:S(2)}, u32[]{:S(2)}) collective-permute-start(bf16[256,256]{1,0:T(8,128)(2,1)} %param.26), channel_id=1, source_target_pairs={{0,30},{2,0},{4,2},{6,4},{8,6},{10,8},{12,10},{14,12},{16,14},{18,... | collective-permute-start | bytes 393224 | tf_op jit(solution)/shard_map/ppermute | solution.py:157
  19.4 1.0 copy.65
  20.4 1.1 convolution_multiply_fusion.4
  21.6 1.6 broadcast_in_dim.66
  25.3 38.6 %all-reduce = bf16[32]{0:T(256)(128)(2,1)S(1)} all-reduce(bf16[32]{0:T(256)(128)(2,1)S(1)} %dynamic-update-slice), channel_id=2, replica_groups=mesh['seq'=16,'head'=2] {'seq'}, use_global_device_ids=true, to_apply=%add | all-reduce | flops 32 | bytes 128
  65.4 5.3 %collective-permute-start.3 = (bf16[256,256]{1,0:T(8,128)(2,1)S(1)}, bf16[256,256]{1,0:T(8,128)(2,1)S(1)}, u32[]{:S(2)}, u32[]{:S(2)}) collective-permute-start(bf16[256,256]{1,0:T(8,128)(2,1)S(1)} %collective-permute-done.1), channel_id=1, source_target_pairs={{0,30},{2,0},{4,2},{6,4},{8,6},{10,8},{12,10},{14,12},{16,14},{18,... | collective-permute-start | bytes 393224 | tf_op jit(solution)/shard_map/ppermute | solution.py:157
  71.4 1.9 collective-permute-done.2
  74.2 5.7 %collective-permute-start.5 = (bf16[256,256]{1,0:T(8,128)(2,1)S(1)}, bf16[256,256]{1,0:T(8,128)(2,1)S(1)}, u32[]{:S(2)}, u32[]{:S(2)}) collective-permute-start(bf16[256,256]{1,0:T(8,128)(2,1)S(1)} %collective-permute-done.3), channel_id=1, source_target_pairs={{0,30},{2,0},{4,2},{6,4},{8,6},{10,8},{12,10},{14,12},{16,14},{18,... | collective-permute-start | bytes 393224 | tf_op jit(solution)/shard_map/ppermute | solution.py:157
  80.6 2.9 collective-permute-done.4
  84.4 5.7 %collective-permute-start.7 = (bf16[256,256]{1,0:T(8,128)(2,1)S(1)}, bf16[256,256]{1,0:T(8,128)(2,1)S(1)}, u32[]{:S(2)}, u32[]{:S(2)}) collective-permute-start(bf16[256,256]{1,0:T(8,128)(2,1)S(1)} %collective-permute-done.5), channel_id=1, source_target_pairs={{0,30},{2,0},{4,2},{6,4},{8,6},{10,8},{12,10},{14,12},{16,14},{18,... | collective-permute-start | bytes 393224 | tf_op jit(solution)/shard_map/ppermute | solution.py:157
  90.8 3.3 collective-permute-done.6
  95.0 5.6 %collective-permute-start.9 = (bf16[256,256]{1,0:T(8,128)(2,1)S(1)}, bf16[256,256]{1,0:T(8,128)(2,1)S(1)}, u32[]{:S(2)}, u32[]{:S(2)}) collective-permute-start(bf16[256,256]{1,0:T(8,128)(2,1)S(1)} %collective-permute-done.7), channel_id=1, source_target_pairs={{0,30},{2,0},{4,2},{6,4},{8,6},{10,8},{12,10},{14,12},{16,14},{18,... | collective-permute-start | bytes 393224 | tf_op jit(solution)/shard_map/ppermute | solution.py:157
  101.4 1.5 collective-permute-done.8
  103.7 1.3 collective-permute-done.9
  105.1 6.2 %collective-permute-start.11 = (bf16[256,256]{1,0:T(8,128)(2,1)S(1)}, bf16[256,256]{1,0:T(8,128)(2,1)S(1)}, u32[]{:S(2)}, u32[]{:S(2)}) collective-permute-start(bf16[256,256]{1,0:T(8,128)(2,1)S(1)} %collective-permute-done.9), channel_id=1, source_target_pairs={{0,30},{2,0},{4,2},{6,4},{8,6},{10,8},{12,10},{14,12},{16,14},{18,... | collective-permute-start | bytes 393224 | tf_op jit(solution)/shard_map/ppermute | solution.py:157
  112.0 1.1 collective-permute-done.10
  114.3 6.2 %collective-permute-start.13 = (bf16[256,256]{1,0:T(8,128)(2,1)S(1)}, bf16[256,256]{1,0:T(8,128)(2,1)S(1)}, u32[]{:S(2)}, u32[]{:S(2)}) collective-permute-start(bf16[256,256]{1,0:T(8,128)(2,1)S(1)} %collective-permute-done.11), channel_id=1, source_target_pairs={{0,30},{2,0},{4,2},{6,4},{8,6},{10,8},{12,10},{14,12},{16,14},{18,... | collective-permute-start | bytes 393224 | tf_op jit(solution)/shard_map/ppermute | solution.py:157
  122.7 2.8 collective-permute-done.13
  126.3 6.9 %collective-permute-done.14 = bf16[256,256]{1,0:T(8,128)(2,1)S(1)} collective-permute-done((bf16[256,256]{1,0:T(8,128)(2,1)S(1)}, bf16[256,256]{1,0:T(8,128)(2,1)S(1)}, u32[]{:S(2)}, u32[]{:S(2)}) %collective-permute-start.14) | collective-permute-done | bytes 131104 | tf_op jit(solution)/shard_map/ppermute | solution.py:148
  134.0 3.4 copy.100
  137.4 4.3 %copy.82 = bf16[32,128,2,128]{3,1,2,0:T(8,128)(2,1)} copy(bf16[32,128,2,128]{1,0,3,2:T(8,128)(2,1)} %bitcast.140) | data formatting | bytes 4194304
  141.8 15.6 %while.39 = (s32[]{:T(128)}, f32[2,128,128]{2,1,0:T(8,128)S(1)}, s32[]{:T(128)}, bf16[16,2]{1,0:T(8,128)(2,1)S(1)}, bf16[16,2,128,128]{3,2,1,0:T(8,128)(2,1)}, /*index=5*/s32[]{:T(128)}, s32[]{:T(128)}) while((s32[]{:T(128)}, f32[2,128,128]{2,1,0:T(8,128)S(1)}, s32[]{:T(128)}, bf16[16,2]{1,0:T(8,128)(2,1)S(1)}, ...), condition=%wide.region_3.4_spmd.clone, body=%wide.region_2.3_spmd.clone.sunk | while | flops 163846 | bytes 327805 | solution.py:31
  141.8 1.0 fusion.77
  143.8 0.9 fusion.77
  158.2 2.1 convolution_convert_fusion.1
  160.4 4.1 %reshape.143 = bf16[32,128,2,128]{3,2,1,0:T(2,128)(2,1)} reshape(bf16[4096,256]{1,0:T(8,128)(2,1)} %all-gather.5.cloned.1.call-done) | data formatting | bytes 4194304 | tf_op jit(solution)/shard_map/reshape | solution.py:168
  164.5 165.0 %while.38 = (s32[]{:T(128)}, f32[2,128]{1,0:T(2,128)S(1)}, f32[2,128]{1,0:T(2,128)S(1)}, f32[128,2,128]{2,0,1:T(8,128)S(1)}, f32[2,128]{1,0:T(2,128)S(1)}, /*ind...) while((s32[]{:T(128)}, f32[2,128]{1,0:T(2,128)S(1)}, ...), condition=%wide.region_23.24_spmd.clone.clone, body=%wide.region_6.23_spmd.clone.clone.sunk | while | flops 34162200 | bytes 2179927 | solution.py:181
  329.8 3.7 convolution_convert_fusion
  333.5 35.3 %reduce-scatter.5.cloned.1.call-done = bf16[256,2048]{1,0:T(8,128)(2,1)} async-done(((bf16[256,4096]{1,0:T(8,128)(2,1)}), bf16[256,2048]{1,0:T(8,128)(2,1)}) %reduce-scatter.5.cloned.1.call-update) | async-done | bytes 1048592 | tf_op jit(solution)/shard_map/reduce_scatter | solution.py:204
  (402 shorter events, 114.9 us)
Async XLA Ops:
  7.2 151.0 %copy-start = (bf16[256,4096]{1,0:T(8,128)(2,1)S(1)}, bf16[256,4096]{1,0:T(8,128)(2,1)}, u32[]{:S(2)}) copy-start(bf16[256,4096]{1,0:T(8,128)(2,1)} %param.28) | copy-start | bytes 6291460
  7.2 134.6 %all-gather.7.cloned.1.call-start = ((), (), s32[]{:S(2)}) async-start(), calls=%async_computation.5 | async-start | bytes 1114112 | tf_op jit(solution)/shard_map/all_gather | solution.py:14
  12.2 148.2 %all-gather.5.cloned.1.call-start = ((), (), s32[]{:S(2)}) async-start(), calls=%async_computation.3 | async-start | bytes 2228224 | tf_op jit(solution)/shard_map/all_gather | solution.py:164
  12.2 51.8 %collective-permute-start = (bf16[256,256]{1,0:T(8,128)(2,1)}, bf16[256,256]{1,0:T(8,128)(2,1)S(1)}, u32[]{:S(2)}, u32[]{:S(2)}) collective-permute-start(bf16[256,256]{1,0:T(8,128)(2,1)} %param.26), channel_id=1, source_target_pairs={{0,2},{2,4},{4,6},{6,8},{8,10},{10,12},{12,14},{14,16},{16,18},{18... | collective-permute-start | bytes 393224 | tf_op jit(solution)/shard_map/ppermute | solution.py:148
  15.2 50.1 %collective-permute-start.1 = (bf16[256,256]{1,0:T(8,128)(2,1)}, bf16[256,256]{1,0:T(8,128)(2,1)S(1)}, u32[]{:S(2)}, u32[]{:S(2)}) collective-permute-start(bf16[256,256]{1,0:T(8,128)(2,1)} %param.26), channel_id=1, source_target_pairs={{0,30},{2,0},{4,2},{6,4},{8,6},{10,8},{12,10},{14,12},{16,14},{18,... | collective-permute-start | bytes 393224 | tf_op jit(solution)/shard_map/ppermute | solution.py:157
  19.3 4.5 %copy-start.2 = (bf16[256,256]{1,0:T(8,128)(2,1)S(1)}, bf16[256,256]{1,0:T(8,128)(2,1)}, u32[]{:S(2)}) copy-start(bf16[256,256]{1,0:T(8,128)(2,1)} %param.25) | copy-start | bytes 393220
  19.3 314.2 %reduce-scatter.3.cloned.1.call-start = ((), (), s32[]{:S(2)}) async-start(), calls=%async_computation.2 | async-start | bytes 3145728 | tf_op jit(solution)/shard_map/reduce_scatter | solution.py:198
  20.4 3.5 copy-start.4
  64.2 9.1 %collective-permute-start.2 = (bf16[256,256]{1,0:T(8,128)(2,1)S(1)}, bf16[256,256]{1,0:T(8,128)(2,1)S(1)}, u32[]{:S(2)}, u32[]{:S(2)}) collective-permute-start(bf16[256,256]{1,0:T(8,128)(2,1)S(1)} %collective-permute-done), channel_id=1, source_target_pairs={{0,2},{2,4},{4,6},{6,8},{8,10},{10,12},{12,14},{14,16},{16,18},{18... | collective-permute-start | bytes 393224 | tf_op jit(solution)/shard_map/ppermute | solution.py:148
  65.4 8.7 %collective-permute-start.3 = (bf16[256,256]{1,0:T(8,128)(2,1)S(1)}, bf16[256,256]{1,0:T(8,128)(2,1)S(1)}, u32[]{:S(2)}, u32[]{:S(2)}) collective-permute-start(bf16[256,256]{1,0:T(8,128)(2,1)S(1)} %collective-permute-done.1), channel_id=1, source_target_pairs={{0,30},{2,0},{4,2},{6,4},{8,6},{10,8},{12,10},{14,12},{16,14},{18,... | collective-permute-start | bytes 393224 | tf_op jit(solution)/shard_map/ppermute | solution.py:157
  73.4 10.1 %collective-permute-start.4 = (bf16[256,256]{1,0:T(8,128)(2,1)S(1)}, bf16[256,256]{1,0:T(8,128)(2,1)S(1)}, u32[]{:S(2)}, u32[]{:S(2)}) collective-permute-start(bf16[256,256]{1,0:T(8,128)(2,1)S(1)} %collective-permute-done.2), channel_id=1, source_target_pairs={{0,2},{2,4},{4,6},{6,8},{8,10},{10,12},{12,14},{14,16},{16,18},{18... | collective-permute-start | bytes 393224 | tf_op jit(solution)/shard_map/ppermute | solution.py:148
  74.2 10.1 %collective-permute-start.5 = (bf16[256,256]{1,0:T(8,128)(2,1)S(1)}, bf16[256,256]{1,0:T(8,128)(2,1)S(1)}, u32[]{:S(2)}, u32[]{:S(2)}) collective-permute-start(bf16[256,256]{1,0:T(8,128)(2,1)S(1)} %collective-permute-done.3), channel_id=1, source_target_pairs={{0,30},{2,0},{4,2},{6,4},{8,6},{10,8},{12,10},{14,12},{16,14},{18,... | collective-permute-start | bytes 393224 | tf_op jit(solution)/shard_map/ppermute | solution.py:157
  83.5 10.5 %collective-permute-start.6 = (bf16[256,256]{1,0:T(8,128)(2,1)S(1)}, bf16[256,256]{1,0:T(8,128)(2,1)S(1)}, u32[]{:S(2)}, u32[]{:S(2)}) collective-permute-start(bf16[256,256]{1,0:T(8,128)(2,1)S(1)} %collective-permute-done.4), channel_id=1, source_target_pairs={{0,2},{2,4},{4,6},{6,8},{8,10},{10,12},{12,14},{14,16},{16,18},{18... | collective-permute-start | bytes 393224 | tf_op jit(solution)/shard_map/ppermute | solution.py:148
  84.4 10.5 %collective-permute-start.7 = (bf16[256,256]{1,0:T(8,128)(2,1)S(1)}, bf16[256,256]{1,0:T(8,128)(2,1)S(1)}, u32[]{:S(2)}, u32[]{:S(2)}) collective-permute-start(bf16[256,256]{1,0:T(8,128)(2,1)S(1)} %collective-permute-done.5), channel_id=1, source_target_pairs={{0,30},{2,0},{4,2},{6,4},{8,6},{10,8},{12,10},{14,12},{16,14},{18,... | collective-permute-start | bytes 393224 | tf_op jit(solution)/shard_map/ppermute | solution.py:157
  94.1 8.7 %collective-permute-start.8 = (bf16[256,256]{1,0:T(8,128)(2,1)S(1)}, bf16[256,256]{1,0:T(8,128)(2,1)S(1)}, u32[]{:S(2)}, u32[]{:S(2)}) collective-permute-start(bf16[256,256]{1,0:T(8,128)(2,1)S(1)} %collective-permute-done.6), channel_id=1, source_target_pairs={{0,2},{2,4},{4,6},{6,8},{8,10},{10,12},{12,14},{14,16},{16,18},{18... | collective-permute-start | bytes 393224 | tf_op jit(solution)/shard_map/ppermute | solution.py:148
  95.0 10.0 %collective-permute-start.9 = (bf16[256,256]{1,0:T(8,128)(2,1)S(1)}, bf16[256,256]{1,0:T(8,128)(2,1)S(1)}, u32[]{:S(2)}, u32[]{:S(2)}) collective-permute-start(bf16[256,256]{1,0:T(8,128)(2,1)S(1)} %collective-permute-done.7), channel_id=1, source_target_pairs={{0,30},{2,0},{4,2},{6,4},{8,6},{10,8},{12,10},{14,12},{16,14},{18,... | collective-permute-start | bytes 393224 | tf_op jit(solution)/shard_map/ppermute | solution.py:157
  103.0 10.2 %collective-permute-start.10 = (bf16[256,256]{1,0:T(8,128)(2,1)S(1)}, bf16[256,256]{1,0:T(8,128)(2,1)S(1)}, u32[]{:S(2)}, u32[]{:S(2)}) collective-permute-start(bf16[256,256]{1,0:T(8,128)(2,1)S(1)} %collective-permute-done.8), channel_id=1, source_target_pairs={{0,2},{2,4},{4,6},{6,8},{8,10},{10,12},{12,14},{14,16},{16,18},{18... | collective-permute-start | bytes 393224 | tf_op jit(solution)/shard_map/ppermute | solution.py:148
  105.1 9.1 %collective-permute-start.11 = (bf16[256,256]{1,0:T(8,128)(2,1)S(1)}, bf16[256,256]{1,0:T(8,128)(2,1)S(1)}, u32[]{:S(2)}, u32[]{:S(2)}) collective-permute-start(bf16[256,256]{1,0:T(8,128)(2,1)S(1)} %collective-permute-done.9), channel_id=1, source_target_pairs={{0,30},{2,0},{4,2},{6,4},{8,6},{10,8},{12,10},{14,12},{16,14},{18,... | collective-permute-start | bytes 393224 | tf_op jit(solution)/shard_map/ppermute | solution.py:157
  113.2 8.6 %collective-permute-start.12 = (bf16[256,256]{1,0:T(8,128)(2,1)S(1)}, bf16[256,256]{1,0:T(8,128)(2,1)S(1)}, u32[]{:S(2)}, u32[]{:S(2)}) collective-permute-start(bf16[256,256]{1,0:T(8,128)(2,1)S(1)} %collective-permute-done.10), channel_id=1, source_target_pairs={{0,2},{2,4},{4,6},{6,8},{8,10},{10,12},{12,14},{14,16},{16,18},{18... | collective-permute-start | bytes 393224 | tf_op jit(solution)/shard_map/ppermute | solution.py:148
  114.3 11.1 %collective-permute-start.13 = (bf16[256,256]{1,0:T(8,128)(2,1)S(1)}, bf16[256,256]{1,0:T(8,128)(2,1)S(1)}, u32[]{:S(2)}, u32[]{:S(2)}) collective-permute-start(bf16[256,256]{1,0:T(8,128)(2,1)S(1)} %collective-permute-done.11), channel_id=1, source_target_pairs={{0,30},{2,0},{4,2},{6,4},{8,6},{10,8},{12,10},{14,12},{16,14},{18,... | collective-permute-start | bytes 393224 | tf_op jit(solution)/shard_map/ppermute | solution.py:157
  122.0 11.3 %collective-permute-start.14 = (bf16[256,256]{1,0:T(8,128)(2,1)S(1)}, bf16[256,256]{1,0:T(8,128)(2,1)S(1)}, u32[]{:S(2)}, u32[]{:S(2)}) collective-permute-start(bf16[256,256]{1,0:T(8,128)(2,1)S(1)} %collective-permute-done.12), channel_id=1, source_target_pairs={{0,2},{2,4},{4,6},{6,8},{8,10},{10,12},{12,14},{14,16},{16,18},{18... | collective-permute-start | bytes 393224 | tf_op jit(solution)/shard_map/ppermute | solution.py:148
  137.4 19.9 %copy-start.3 = (bf16[256,256]{1,0:T(8,128)(2,1)S(1)}, bf16[256,256]{1,0:T(8,128)(2,1)}, u32[]{:S(2)}) copy-start(bf16[256,256]{1,0:T(8,128)(2,1)} %param.21) | copy-start | bytes 393220
  141.8 15.9 %copy-start.1 = (bf16[256,256]{1,0:T(8,128)(2,1)S(1)}, bf16[256,256]{1,0:T(8,128)(2,1)}, u32[]{:S(2)}) copy-start(bf16[256,256]{1,0:T(8,128)(2,1)} %param.23) | copy-start | bytes 393220
  160.3 208.5 %reduce-scatter.5.cloned.1.call-start = ((), (), s32[]{:S(2)}) async-start(), calls=%async_computation.4 | async-start | bytes 3145728 | tf_op jit(solution)/shard_map/reduce_scatter | solution.py:204
Sparse Core Ops, SparseCore 0:
  12.3 60.2 all-gather.6
  75.3 63.9 all-gather.4
  160.4 5.4 reduce-scatter.2
  333.6 35.1 reduce-scatter.4
